TPU v7x, 512 devices: a whole 4x4x16 slice. The times are simulated.
512 devices in a mesh: dp: 32 (over x, y, core), mp: 16 (over z).
Axes of the slice: x: 4, y: 4, z: 16, core: 2. Of those that a mesh axis runs over, the one named last changes fastest.
Arguments:
- activations: bfloat16 [4096, 8192], P('mp', 'dp'), may hold values from -600 to 600
- out_grads: bfloat16 [4096, 28672], P('dp', 'mp'), may hold values from -1 to 1
- row_moment: float32 [8192], P('dp'), may hold values from 0.003 to 0.3
- col_moment: float32 [28672], P('mp'), may hold values from 0.003 to 0.3
Outputs:
- update: float32 [8192, 28672], P('dp', 'mp')
- new_rows: float32 [8192], P('dp')
- new_cols: float32 [28672], P('mp')
All inputs are finite; a program needn't handle non-finite values.
Results may differ from a plain program's by a relative error of at most 0.0003.
Values may be sent and summed in bfloat16 or wider, within the bound.
A program may use at most 64 MiB of HBM per device.

v0:
```python
import jax
import jax.numpy as jnp
from jax import lax
from jax.sharding import PartitionSpec as P

decay_rate = 0.8
clip_bound = 1.0


def contract(left, right):
    return lax.dot_general(
        left, right, (((0,), (0,)), ((), ())), preferred_element_type=jnp.float32
    )


def shards(activations, out_grads, row_moment, col_moment):
    local_rows = activations.shape[1]
    local_cols = out_grads.shape[1]
    all_rows = local_rows * lax.axis_size("dp")
    all_cols = local_cols * lax.axis_size("mp")
    whole_inputs = lax.all_gather(activations, "mp", axis=0, tiled=True)
    gradient = contract(whole_inputs, lax.all_gather(out_grads, "dp", axis=0, tiled=True))
    squares = gradient * gradient
    row_part = jnp.sum(squares, axis=1)
    col_part = jnp.sum(squares, axis=0)
    row_total = lax.psum(row_part, "mp")
    col_total = lax.psum(col_part, "dp")
    new_rows = decay_rate * row_moment + (1.0 - decay_rate) * (row_total / all_cols)
    new_cols = decay_rate * col_moment + (1.0 - decay_rate) * (col_total / all_rows)
    scaled = gradient * lax.rsqrt(new_rows)[:, None] * lax.rsqrt(new_cols)[None, :]
    clip_total = lax.psum(jnp.sum(scaled * scaled), ("dp", "mp"))
    root_mean = jnp.sqrt(clip_total / (all_rows * all_cols))
    update = scaled / jnp.maximum(1.0, root_mean / clip_bound)
    return (update, new_rows, new_cols)


def solution(mesh):
    placed = (P("mp", "dp"), P("dp", "mp"), P("dp"), P("mp"))
    return jax.shard_map(
        shards,
        mesh=mesh,
        in_specs=placed,
        out_specs=(P("dp", "mp"), P("dp"), P("mp")),
        check_vma=False,
    )
```

profile of v0, /device:TPU:1, one launch (start us, length us, event | category | flops | bytes accessed | tf_op | source)
XLA Modules:
  0.0 386.2 jit_solution(2357931704904544405)
XLA Ops:
  7.2 0.0 all-gather.3.cloned.1.call-start
  7.2 0.7 all-gather.3.cloned.1.call-update
  7.9 0.0 all-gather.5.cloned.1.call-start
  7.9 0.7 all-gather.5.cloned.1.call-update
  8.6 0.0 copy-start.1
  8.7 0.0 copy-start
  8.7 70.8 %all-gather.3.cloned.1.call-done = bf16[4096,256]{1,0:T(8,128)(2,1)} async-done(((bf16[256,256]{1,0:T(8,128)(2,1)}), bf16[4096,256]{1,0:T(8,128)(2,1)}) %all-gather.3.cloned.1.call-update) | async-done | bytes 2097168 | tf_op jit(solution)/shard_map/all_gather | solution.py:21
  79.5 92.7 %all-gather.5.cloned.1.call-done = bf16[4096,1792]{1,0:T(8,128)(2,1)} async-done(((bf16[128,1792]{1,0:T(8,128)(2,1)}), bf16[4096,1792]{1,0:T(8,128)(2,1)}) %all-gather.5.cloned.1.call-update) | async-done | bytes 14680080 | tf_op jit(solution)/shard_map/all_gather | solution.py:22
  172.2 8.6 %multiply_reduce_fusion.2 = (f32[256]{0:T(256)S(1)}, f32[1792]{0:T(1024)S(1)}, f32[256,1792]{1,0:T(8,128)S(1)}) fusion(bf16[4096,256]{1,0:T(8,128)(2,1)} %all-gather.3.cloned.1.call-done, bf16[4096,1792]{1,0:T(8,128)(2,1)} %all-gather.5.cloned.1.call-done), kind=kOutput, calls=%fused_computation.3 | convolution fusion | flops 3759470592 | bytes 18620416 | tf_op jit(solution)/shard_map/dot_general | solution.py:11
  180.8 24.7 %psum.21 = f32[256]{0:T(256)S(1)} all-reduce(f32[256]{0:T(256)S(1)} %get-tuple-element.3), channel_id=1, replica_groups=mesh['dp'=32,'mp'=16] {'mp'}, use_global_device_ids=true, to_apply=%region_1.0 | all-reduce | flops 256 | bytes 2048 | tf_op jit(solution)/shard_map/psum | solution.py:26
  205.5 69.8 %psum.22 = f32[1792]{0:T(1024)S(1)} all-reduce(f32[1792]{0:T(1024)S(1)} %get-tuple-element.4), channel_id=1, replica_groups=mesh['dp'=32,'mp'=16] {'dp'}, use_global_device_ids=true, to_apply=%region_3.0 | all-reduce | flops 1792 | bytes 14336 | tf_op jit(solution)/shard_map/psum | solution.py:27
  275.3 0.0 copy-done.1
  275.3 0.6 fusion.1
  275.9 0.0 copy-done
  275.9 0.6 fusion.2
  276.5 1.3 multiply_reduce_fusion
  277.8 99.4 %psum.23 = f32[]{:T(128)} all-reduce(f32[]{:T(128)} %multiply_reduce_fusion), channel_id=1, replica_groups=mesh['dp'=32,'mp'=16] {'dp','mp'}, use_global_device_ids=true, to_apply=%region_5.0 | all-reduce | flops 1 | bytes 8 | tf_op jit(solution)/shard_map/psum | solution.py:31
  377.9 1.5 fusion
Async XLA Ops:
  7.2 72.3 %all-gather.3.cloned.1.call-start = ((), (), s32[]{:S(2)}) async-start(), calls=%async_computation | async-start | bytes 2228224 | tf_op jit(solution)/shard_map/all_gather | solution.py:21
  7.9 164.3 %all-gather.5.cloned.1.call-start = ((), (), s32[]{:S(2)}) async-start(), calls=%async_computation.1 | async-start | bytes 15138816 | tf_op jit(solution)/shard_map/all_gather | solution.py:22
  8.6 266.7 %copy-start.1 = (f32[256]{0:T(256)S(1)}, f32[256]{0:T(256)}, u32[]{:S(2)}) copy-start(f32[256]{0:T(256)} %param.6) | copy-start | bytes 3076
  8.7 267.3 %copy-start = (f32[1792]{0:T(1024)S(1)}, f32[1792]{0:T(1024)}, u32[]{:S(2)}) copy-start(f32[1792]{0:T(1024)} %param.7) | copy-start | bytes 21508
Sparse Core Ops, SparseCore 0:
  10.1 69.3 all-gather.2
  82.6 89.5 all-gather.4
where the time goes:
time: 387 us; the launch traced here: 386 us
  blocking collectives  194 us (50%)
  waiting for transfers between devices  165 us (43%)
  between operations  14.8 us (4%)
  matrix products  8.63 us (2%)
  other arithmetic  3.94 us (1%)
    psum x1, blocking collectives, shards(): clip_total = lax.psum(jnp.sum(scaled * scaled), ('dp', 'mp'))  99.4 us
    all_gather x1, waiting for transfers between devices, shards(): lax.all_gather(out_grads, 'dp', axis=0, tiled=True)  92.7 us
    all_gather x1, waiting for transfers between devices, shards(): whole_inputs = lax.all_gather(activations, 'mp', axis=0, tiled=True)  70.8 us
    psum x1, blocking collectives, shards(): col_total = lax.psum(col_part, 'dp')  69.8 us
    psum x1, blocking collectives, shards(): row_total = lax.psum(row_part, 'mp')  24.7 us
    dot_general x1, matrix products, contract(): lax.dot_general(left, right, (((0,), (0,)), ((), ())), preferred_element_...  8.63 us
  transfers between devices with their start and end apart: 2, of which 2 were waited for; matrix products, arithmetic and copies ran while one was open for 0% of the time, Pallas kernels for 0%

commit v1 on v0

v1 whole, which is shorter than its diff:
```python
import functools

import jax
import jax.numpy as jnp
from jax import lax
from jax.experimental import pallas as pl
from jax.experimental.pallas import tpu as pltpu
from jax.sharding import PartitionSpec as P

decay_rate = 0.8
clip_bound = 1.0

MESH = pl.DeviceIdType.MESH
SIDE = 4
DEEP = 16
TILE = 256
PASSES = (2, 2, 2, 1)


def near(d):
    d = d % SIDE
    return d - SIDE if d == SIDE - 1 else d


def piece_names():
    names = []
    for half in range(2):
        for v in (0, -1, 1, 2):
            for u in (0, -1, 1, 2):
                if (u, v) == (0, 0):
                    continue
                last = u if v == 0 else v
                names += [(half, u, v, part) for part in (("a", "b") if last == 2 else ("f",))]
    return names


PIECES = {name: i for i, name in enumerate(piece_names())}


def exchange(
    act_ref, grad_ref, row_ref, col_ref,
    out_ref, rows_out, cols_out, clip_out,
    act, a_all, a_send, g_all, part, part_in, cols_mine, cols_core, cols_x, cols_y, cols_all, late, row_acc, z_all, clip_all,
    local_sem, a_send_sem, a_recv_sem, g_send_sem, g_recv_sem, core_send_sem, core_recv_sem,
    part_send_sem, part_recv_sem, x_send_sem, x_recv_sem, y_send_sem, y_recv_sem,
    late_send_sem, late_recv_sem, z_send_sem, z_recv_sem, clip_send_sem, clip_recv_sem,
):
    me, z = lax.axis_index("dp"), lax.axis_index("mp")
    x, y, core = me // 8, (me // 2) % SIDE, me % 2
    rows, tokens = act_ref.shape[1], grad_ref.shape[0]
    part_rows = tokens // 2
    tiles = sum(PASSES)
    early = sum(PASSES[:-1])

    def device(dx, dy, dc, dz):
        there = (((x + dx) % SIDE) * SIDE + (y + dy) % SIDE) * 2 + (core + dc) % 2
        return there, (z + dz) % DEEP

    def chip(dx, dy):
        return ((x + dx) % SIDE) * SIDE + (y + dy) % SIDE

    def remote(src, dst, send, recv, where):
        return pltpu.make_async_remote_copy(
            src_ref=src, dst_ref=dst, send_sem=send, recv_sem=recv,
            device_id=device(*where), device_id_type=MESH,
        )

    load_act = pltpu.make_async_copy(act_ref, act, local_sem.at[0])
    load_grad = pltpu.make_async_copy(grad_ref, g_all.at[chip(0, 0)], local_sem.at[1])
    load_grad.start()
    load_act.start()

    neighbours = [(1, 0, 0, 0), (-1, 0, 0, 0), (0, 1, 0, 0), (0, -1, 0, 0), (0, 0, 1, 0), (0, 0, 0, 1), (0, 0, 0, -1)]
    barrier = pltpu.get_barrier_semaphore()
    for where in neighbours:
        pl.semaphore_signal(barrier, inc=1, device_id=device(*where), device_id_type=MESH)
    load_grad.wait()
    pl.semaphore_wait(barrier, len(neighbours))

    starts = [sum(PASSES[:p]) * TILE for p in range(len(PASSES))]

    def g_piece(step, half, u, v, part_name):
        dx, dy = (u, v) if half == 0 else (v, u)
        offset, height = {"f": (0, part_rows), "a": (0, part_rows // 2), "b": (part_rows // 2, part_rows // 2)}[part_name]
        return g_all.at[
            chip(dx, dy),
            pl.ds(half * part_rows + offset, height),
            pl.ds(starts[step], PASSES[step] * TILE),
        ]

    def g_copy(step, half, u, v, part_name, axis, way):
        du, dv = (way, 0) if axis == 0 else (0, way)
        name = (half, near(u - du), near(v - dv), part_name)
        dx, dy = (du, dv) if half == 0 else (dv, du)
        ref = g_piece(step, half, u, v, part_name)
        return remote(ref, ref, g_send_sem, g_recv_sem.at[step, PIECES[name]], (dx, dy, 0, 0))

    def g_wait(step, half, u, v, part_name):
        ref = g_piece(step, half, u, v, part_name)
        pltpu.make_async_copy(ref, ref, g_recv_sem.at[step, PIECES[(half, u, v, part_name)]]).wait()

    def spread(step, half, u):
        for way in (1, -1):
            g_copy(step, half, u, 0, "f", 1, way).start()

    def own(step):
        def run():
            for half in range(2):
                for way in (1, -1):
                    g_copy(step, half, 0, 0, "f", 0, way).start()
            for half in range(2):
                spread(step, half, 0)

        return [run]

    def first(step):
        def run(half, u):
            g_wait(step, half, u, 0, "f")
            g_copy(step, half, u, 0, "a" if u < 0 else "b", 0, -u).start()
            spread(step, half, u)

        return [functools.partial(run, half, u) for u in (-1, 1) for half in range(2)]

    def opposite(step):
        def run(half):
            g_wait(step, half, 2, 0, "a")
            g_wait(step, half, 2, 0, "b")
            spread(step, half, 2)

        return [functools.partial(run, half) for half in range(2)]

    def second(step, u):
        def run(half, v):
            g_wait(step, half, u, v, "f")
            g_copy(step, half, u, v, "a" if v < 0 else "b", 1, -v).start()

        return [functools.partial(run, half, v) for v in (-1, 1) for half in range(2)]

    def final(step):
        def run(half, u):
            g_wait(step, half, u, 2, "a")
            g_wait(step, half, u, 2, "b")

        return [functools.partial(run, half, u) for u in (0, -1, 1, 2) for half in range(2)]

    def a_piece(kind, dz):
        owner = core if kind == 0 else 1 - core
        return a_all.at[owner, :, pl.ds(pl.multiple_of(((z + dz) % DEEP) * tokens, tokens), tokens)]

    def a_copy(kind, dz, way):
        ref = a_piece(kind, dz)
        return remote(ref, ref, a_send_sem, a_recv_sem.at[kind, (dz - way) % DEEP], (0, 0, 0, way))

    def a_reach(kind, way):
        return DEEP // 2 if (kind == 0) == (way == 1) else DEEP // 2 - 1

    def a_step(kind, way, far):
        dz = -way * far
        ref = a_piece(kind, dz)
        pltpu.make_async_copy(ref, ref, a_recv_sem.at[kind, dz % DEEP]).wait()
        if far < a_reach(kind, way):
            a_copy(kind, dz, way).start()

    def a_swap():
        return remote(
            a_send, a_all.at[core, :, pl.ds(pl.multiple_of(z * tokens, tokens), tokens)],
            core_send_sem.at[0], core_recv_sem.at[0], (0, 0, 1, 0),
        )

    def a_own():
        load_act.wait()
        turned = act[...].T
        lower, upper = turned[:, :tokens], turned[:, tokens:]
        a_all[core, :, pl.ds(pl.multiple_of(z * tokens, tokens), tokens)] = jnp.where(core == 0, lower, upper)
        a_send[...] = jnp.where(core == 0, upper, lower)
        a_swap().start()
        for way in (1, -1):
            a_copy(0, 0, way).start()

    def a_other():
        ref = a_piece(1, 0)
        pltpu.make_async_copy(ref, ref, core_recv_sem.at[0]).wait()
        for way in (1, -1):
            a_copy(1, 0, way).start()

    a_events = [a_own, a_other]
    for far in range(1, DEEP // 2 + 1):
        for kind in range(2):
            for way in (1, -1):
                if far <= a_reach(kind, way):
                    a_events.append(functools.partial(a_step, kind, way, far))

    def part_copy(t):
        return remote(part.at[t, 1 - core], part_in.at[t], part_send_sem.at[t], part_recv_sem.at[t], (0, 0, 1, 0))

    def product(t):
        left = a_all[...].reshape(2 * rows, DEEP * tokens)
        right = g_all[:, :, pl.ds(t * TILE, TILE)].reshape(DEEP * tokens, TILE)
        value = jnp.dot(left, right, preferred_element_type=jnp.float32)
        part[t] = value.reshape(2, rows, TILE)
        part_copy(t).start()

    def squares(t):
        block = out_ref[:, pl.ds(t * TILE, TILE)]
        return block * block

    def lanes(block):
        return sum(block[:, i * 128 : (i + 1) * 128] for i in range(TILE // 128))

    def joined(t):
        part_copy(t).wait_recv()
        out_ref[:, pl.ds(t * TILE, TILE)] = part[t, core] + part_in[t]
        square = squares(t)
        if t == 0:
            row_acc[0] = lanes(square)
        else:
            row_acc[0] = row_acc[0] + lanes(square)
        total = jnp.sum(square, axis=0, keepdims=True)
        if t < early:
            cols_mine[:, pl.ds(t * TILE, TILE)] = total
        else:
            late[me] = total

    def core_copy():
        return remote(cols_mine, cols_core, core_send_sem.at[1], core_recv_sem.at[1], (0, 0, 1, 0))

    def x_copy(k):
        return remote(cols_x.at[x], cols_x.at[x], x_send_sem.at[k], x_recv_sem.at[k], (k, 0, 0, 0))

    def x_wait(k):
        ref = cols_x.at[(x - k) % SIDE]
        pltpu.make_async_copy(ref, ref, x_recv_sem.at[k]).wait()

    def y_copy(k):
        return remote(cols_y.at[y], cols_y.at[y], y_send_sem.at[k], y_recv_sem.at[k], (0, k, 0, 0))

    def y_wait(k):
        ref = cols_y.at[(y - k) % SIDE]
        pltpu.make_async_copy(ref, ref, y_recv_sem.at[k]).wait()

    def cols_1():
        core_copy().start()

    def cols_2():
        core_copy().wait_recv()
        cols_x[x] = cols_mine[...] + cols_core[...]
        for k in (2, 1, 3):
            x_copy(k).start()

    def cols_3():
        for k in (1, 3, 2):
            x_wait(k)
        cols_y[y] = (cols_x[0] + cols_x[1]) + (cols_x[2] + cols_x[3])
        for k in (2, 1, 3):
            y_copy(k).start()

    def cols_4():
        for k in (1, 3, 2):
            y_wait(k)
        cols_all[:, pl.ds(0, early * TILE)] = (cols_y[0] + cols_y[1]) + (cols_y[2] + cols_y[3])

    last = len(PASSES) - 1
    order = []

    def put(events):
        for event in events:
            order.append(event)

    put(own(0))
    put([a_events.pop(0)])
    put(first(0))
    put(opposite(0))
    for step in range(last + 1):
        if step < last:
            put(own(step + 1))
        put(second(step, 0))
        put(second(step, -1))
        put(second(step, 1))
        if step < last:
            put(first(step + 1))
        put(second(step, 2))
        if step < last:
            put(opposite(step + 1))
        put(final(step))
        put([("pass", step)])

    count, ready, pending, chain = 0, [], [], [cols_1, cols_2, cols_3, cols_4]
    left_early = list(range(early))

    def join():
        t = pending.pop(0)
        joined(t)
        left_early.remove(t)

    def work():
        if a_events:
            return
        if ready and ready[0] < early:
            t = ready.pop(0)
            product(t)
            pending.append(t)
            if len(pending) > 1:
                join()
        elif pending:
            join()
        elif chain and not left_early:
            chain.pop(0)()

    for event in order:
        if isinstance(event, tuple):
            t0 = sum(PASSES[: event[1]])
            ready += range(t0, t0 + PASSES[event[1]])
            continue
        event()
        count += 1
        if a_events:
            if count % 2 == 0:
                a_events.pop(0)()
        elif count % 3 == 0:
            work()
    while a_events:
        a_events.pop(0)()
    while left_early:
        work()
    while len(chain) > 2:
        chain.pop(0)()
    for t in range(early, tiles):
        product(t)
    for t in range(early, tiles):
        joined(t)

    peers = [(dx, dy, dc) for dx in range(SIDE) for dy in range(SIDE) for dc in range(2) if (dx, dy, dc) != (0, 0, 0)]
    peers.sort(key=lambda p: -(min(p[0], SIDE - p[0]) + min(p[1], SIDE - p[1])))

    def from_peer(dx, dy, dc):
        return (((x - dx) % SIDE) * SIDE + (y - dy) % SIDE) * 2 + (core - dc) % 2

    def late_copy(i):
        return remote(late.at[me], late.at[me], late_send_sem.at[i], late_recv_sem.at[i], (*peers[i], 0))

    for i in range(len(peers)):
        late_copy(i).start()

    def flat(block):
        return jnp.sum(block.T, axis=0, keepdims=True)

    z_all[z, :, pl.ds(0, rows)] = flat(row_acc[0])
    while chain:
        chain.pop(0)()
    all_rows = rows * lax.axis_size("dp")
    all_cols = tiles * TILE * lax.axis_size("mp")

    def new_cols(t):
        span = pl.ds(t * TILE, TILE)
        return decay_rate * col_ref[:, span] + (1.0 - decay_rate) * (cols_all[:, span] / all_rows)

    for t in range(early):
        term = lanes(squares(t) * (1.0 / new_cols(t)))
        row_acc[1] = term if t == 0 else row_acc[1] + term
    for i, peer in enumerate(peers):
        ref = late.at[from_peer(*peer)]
        pltpu.make_async_copy(ref, ref, late_recv_sem.at[i]).wait()
    cols_all[:, pl.ds(early * TILE, (tiles - early) * TILE)] = jnp.sum(late[...], axis=0)
    for t in range(early, tiles):
        row_acc[1] = row_acc[1] + lanes(squares(t) * (1.0 / new_cols(t)))
    z_all[z, :, pl.ds(rows, rows)] = flat(row_acc[1])

    deep = sorted(range(1, DEEP), key=lambda k: -min(k, DEEP - k))

    def z_copy(i):
        return remote(z_all.at[z], z_all.at[z], z_send_sem.at[i], z_recv_sem.at[i], (0, 0, 0, deep[i]))

    for i in range(len(deep)):
        z_copy(i).start()
    cols_out[...] = cols_all[...]
    for i, k in enumerate(deep):
        ref = z_all.at[(z - k) % DEEP]
        pltpu.make_async_copy(ref, ref, z_recv_sem.at[i]).wait()
    sums = jnp.sum(z_all[...], axis=0)
    row_total = sums[:, :rows]
    new_rows = decay_rate * row_ref[...] + (1.0 - decay_rate) * (row_total / all_cols)
    share = sums[:, rows:] / new_rows
    clip_all[me] = sum(share[:, i * 128 : (i + 1) * 128] for i in range(rows // 128))

    def clip_copy(i):
        return remote(clip_all.at[me], clip_all.at[me], clip_send_sem.at[i], clip_recv_sem.at[i], (*peers[i], 0))

    for i in range(len(peers)):
        clip_copy(i).start()
    rows_out[...] = row_total
    sent = a_all.at[:, :, pl.ds(0, (DEEP - 1) * tokens)]
    pltpu.make_async_copy(sent, sent, a_send_sem).wait()
    sent = g_all.at[pl.ds(0, SIDE * SIDE - 1)]
    pltpu.make_async_copy(sent, sent, g_send_sem).wait()
    a_swap().wait_send()
    core_copy().wait_send()
    for k in range(1, SIDE):
        x_copy(k).wait_send()
        y_copy(k).wait_send()
    for t in range(tiles):
        part_copy(t).wait_send()
    for i in range(len(peers)):
        late_copy(i).wait_send()
    for i in range(len(deep)):
        z_copy(i).wait_send()
    for i, peer in enumerate(peers):
        ref = clip_all.at[from_peer(*peer)]
        pltpu.make_async_copy(ref, ref, clip_recv_sem.at[i]).wait()
    clip_out[...] = jnp.sum(clip_all[...], axis=0)
    for i in range(len(peers)):
        clip_copy(i).wait_send()


def finish(all_rows, all_cols, g_ref, rows_ref, cols_ref, clip_ref, row_ref, col_ref, out_ref, new_rows_ref, new_cols_ref, scale):
    rows = g_ref.shape[0]

    @pl.when(pl.program_id(0) == 0)
    def _():
        new_rows = decay_rate * row_ref[...] + (1.0 - decay_rate) * (rows_ref[...] / all_cols)
        new_rows_ref[...] = new_rows
        new_cols_ref[...] = decay_rate * col_ref[...] + (1.0 - decay_rate) * (cols_ref[...] / all_rows)
        total = jnp.sum(clip_ref[...], axis=1, keepdims=True)
        root_mean = jnp.sqrt(total / (all_rows * all_cols))
        factor = lax.rsqrt(new_rows) / jnp.maximum(1.0, root_mean / clip_bound)
        scale[...] = jnp.broadcast_to(factor, (128, rows)).T

    height = out_ref.shape[0]
    here = pl.ds(pl.multiple_of(pl.program_id(0) * height, height), height)
    weight = lax.rsqrt(new_cols_ref[...])
    for i in range(g_ref.shape[1] // 128):
        span = slice(i * 128, (i + 1) * 128)
        out_ref[:, span] = g_ref[here, span] * scale[here, :] * weight[:, span]


def shards(activations, out_grads, row_moment, col_moment):
    rows, tokens, columns = activations.shape[1], out_grads.shape[0], out_grads.shape[1]
    devices = lax.axis_size("dp")
    all_rows, all_cols = rows * devices, columns * lax.axis_size("mp")
    tiles = columns // TILE
    early = sum(PASSES[:-1]) * TILE
    f32, bf16 = jnp.float32, jnp.bfloat16
    vmem, anywhere = pl.BlockSpec(memory_space=pltpu.VMEM), pl.BlockSpec(memory_space=pl.ANY)
    dma = pltpu.SemaphoreType.DMA
    row_moment, col_moment = row_moment[None, :], col_moment[None, :]
    gradient, row_total, col_total, clip = pl.pallas_call(
        exchange,
        name="exchange",
        out_shape=(
            pltpu.VMEM((rows, columns), f32),
            jax.ShapeDtypeStruct((1, rows), f32),
            jax.ShapeDtypeStruct((1, columns), f32),
            jax.ShapeDtypeStruct((1, 128), f32),
        ),
        in_specs=[anywhere, anywhere, vmem, vmem],
        out_specs=(vmem,) * 4,
        scratch_shapes=[
            pltpu.VMEM((2 * tokens, rows), bf16),
            pltpu.VMEM((2, rows, DEEP * tokens), bf16),
            pltpu.VMEM((rows, tokens), bf16),
            pltpu.VMEM((SIDE * SIDE, tokens, columns), bf16),
            pltpu.VMEM((tiles, 2, rows, TILE), f32),
            pltpu.VMEM((tiles, rows, TILE), f32),
            pltpu.VMEM((1, early), f32),
            pltpu.VMEM((1, early), f32),
            pltpu.VMEM((SIDE, 1, early), f32),
            pltpu.VMEM((SIDE, 1, early), f32),
            pltpu.VMEM((1, columns), f32),
            pltpu.VMEM((devices, 1, columns - early), f32),
            pltpu.VMEM((2, rows, 128), f32),
            pltpu.VMEM((DEEP, 1, 2 * rows), f32),
            pltpu.VMEM((devices, 1, 128), f32),
            dma((2,)),
            dma,
            dma((2, DEEP)),
            dma,
            dma((len(PASSES), len(PIECES))),
            dma((2,)),
            dma((2,)),
            dma((tiles,)),
            dma((tiles,)),
            dma((SIDE,)),
            dma((SIDE,)),
            dma((SIDE,)),
            dma((SIDE,)),
            dma((devices - 1,)),
            dma((devices - 1,)),
            dma((DEEP - 1,)),
            dma((DEEP - 1,)),
            dma((devices - 1,)),
            dma((devices - 1,)),
        ],
        compiler_params=pltpu.CompilerParams(
            collective_id=0, has_side_effects=True, vmem_limit_bytes=40 << 20
        ),
        cost_estimate=pl.CostEstimate(
            flops=2 * rows * columns * tokens * devices, bytes_accessed=4 * rows * columns, transcendentals=0
        ),
    )(activations, out_grads, row_moment, col_moment)
    height = 64
    update, new_rows, new_cols = pl.pallas_call(
        functools.partial(finish, all_rows, all_cols),
        name="finish",
        grid=(rows // height,),
        out_shape=(
            jax.ShapeDtypeStruct((rows, columns), f32),
            jax.ShapeDtypeStruct((1, rows), f32),
            jax.ShapeDtypeStruct((1, columns), f32),
        ),
        in_specs=[vmem] * 6,
        out_specs=(pl.BlockSpec((height, columns), lambda i: (i, 0)), vmem, vmem),
        scratch_shapes=[pltpu.VMEM((rows, 128), f32)],
        compiler_params=pltpu.CompilerParams(vmem_limit_bytes=16 << 20),
    )(gradient, row_total, col_total, clip, row_moment, col_moment)
    return update, new_rows[0], new_cols[0]


def solution(mesh):
    placed = (P("mp", "dp"), P("dp", "mp"), P("dp"), P("mp"))
    return jax.shard_map(
        shards,
        mesh=mesh,
        in_specs=placed,
        out_specs=(P("dp", "mp"), P("dp"), P("mp")),
        check_vma=False,
    )
```

time: 387 us -> 104 us (0.27)
  blocking collectives: 194 us -> 0 us
  waiting for transfers between devices: 165 us -> 0 us
  Pallas kernels: 0 us -> 98.7 us
  between operations: 14.8 us -> 0.64 us
  matrix products: 8.63 us -> 0 us
    psum x3 -> x0, blocking collectives: 194 us -> none  [the longest x1 99.4 us: shards(): clip_total = lax.psum(jnp.sum(scaled * scaled), ('dp', 'mp'))]
    all_gather x2 -> x0, waiting for transfers between devices: 163 us -> none  [the longest x1 92.7 us: shards(): lax.all_gather(out_grads, 'dp', axis=0, tiled=True)]
    pallas_call x0 -> x2, Pallas kernels: none -> 98.7 us  [the longest x1 96.7 us: shards(): pl.pallas_call(exchange, name='exchange', out_shape=(pltpu.VMEM((rows, co...]
    dot_general x1 -> x0, matrix products: 8.63 us -> none  [contract(): lax.dot_general(left, right, (((0,), (0,)), ((), ())), preferred_element_...]
  transfers between devices with their start and end apart: 2 -> 0, of which waited for: 2 -> 0; matrix products, arithmetic and copies ran while one was open for 0% -> 0% of each run, Pallas kernels for 0% -> 0%
where the time goes in v1:
time: 104 us; the launch traced here: 103 us
  Pallas kernels  98.7 us (95%)
  local copies, waits for them, and re-layouts  3.3 us (3%)
    pallas_call x1, Pallas kernels, shards(): pl.pallas_call(exchange, name='exchange', out_shape=(pltpu.VMEM((rows, co...  96.7 us
    unnamed x6, local copies, waits for them, and re-layouts  2.6 us

profile of v1, /device:TPU:1, one launch (start us, length us, event | category | flops | bytes accessed | tf_op | source)
XLA Modules:
  0.0 103.3 jit_solution(304603443897991921)
XLA Ops:
  0.6 0.7 broadcast_in_dim.7.col_ref
  1.3 0.0 copy-start
  1.3 0.7 copy-done
  2.0 0.0 copy-start.1
  2.0 1.0 copy-done.1
  3.0 0.0 copy-start.2
  3.0 0.9 copy-done.2
  3.9 96.7 %exchange.1 = (f32[256,1792]{1,0:T(8,128)S(1)}, f32[1,256]{1,0:T(1,128)S(1)}, f32[1,1792]{1,0:T(1,128)S(1)}, f32[1,128]{1,0:T(1,128)S(1)}) custom-call(bf16[256,256]{1,0:T(8,128)(2,1)S(1)} %copy-done.2, bf16[128,1792]{1,0:T(8,128)(2,1)S(1)} %copy-done.1, f32[1,256]{1,0:T(1,128)S(1)} %bitcast.2, f32[1,1792]{1,0:T(1,128)S(1)} %broadcast_in_dim.7.col_ref), custom_call_target="tpu_custom_call" | custom-call | flops 3758096384 | bytes 1835008 | tf_op jit(solution)/shard_map/exchange/pallas_call | solution.py:445
  100.7 2.0 %finish.1 = (f32[256,1792]{1,0:T(8,128)}, f32[1,256]{1,0:T(1,128)}, f32[1,1792]{1,0:T(1,128)S(1)}) custom-call(f32[256,1792]{1,0:T(8,128)S(1)} %get-tuple-element.10.g_ref, f32[1,256]{1,0:T(1,128)S(1)} %get-tuple-element.11.rows_ref, f32[1,1792]{1,0:T(1,128)S(1)} %get-tuple-element.12.cols_ref, f32[1,128]{1,0:T(1,128)S(1)} %get-tuple-element.13.clip_ref, ...), custom_call_target="tpu_custom_call" | custom-call | tf_op jit(solution)/shard_map/finish/pallas_call | solution.py:500
  102.7 0.6 reduce
Async XLA Ops:
  1.3 0.7 copy-start
  2.0 1.0 copy-start.1
  3.0 0.9 copy-start.2
